TPU v7x, 128 devices: a whole 4x4x4 slice. The times are simulated.
128 devices in a mesh: face: 8 (over z_lo, x), tile: 16 (over z_hi, y, core).
Axes of the slice: x: 4, y: 4, z: 4 (z_hi: 2, z_lo: 2; z = z_hi * 2 + z_lo), core: 2. Of those that a mesh axis runs over, the one named last changes fastest.
Arguments:
- source: bfloat16 [8192, 16, 128], P(('face', 'tile')), may hold values from -6 to 6
- entry_block: int32 [16384], P(('face', 'tile')), may hold values from 0 to 16383, as said below
- entry_source: int32 [16384], P(('face', 'tile')), may hold values from 0 to 63
- entry_weight: bfloat16 [16384, 128, 128], P(('face', 'tile')), may hold values from -0.5 to 0.5
- lat_to_nested: int32 [16384], P(('face', 'tile')), may hold values from 0 to 16383, as said below
- face_links: int32 [8, 4, 3], replicated, may hold values from 0 to 7, as said below
- w_in: bfloat16 [16, 90], replicated, may hold values from -1.5 to 1.5
- b_in: float32 [90], replicated, may hold values from -3 to 3
- kernel: float32 [9, 90], replicated, may hold values from -2 to 2
- ln_gain: float32 [90], replicated, may hold values from 0.1 to 1.9
- ln_bias: float32 [90], replicated, may hold values from -3 to 3
- w_one: bfloat16 [90, 360], replicated, may hold values from -0.625 to 0.625
- b_one: float32 [360], replicated, may hold values from -3 to 3
- w_two: bfloat16 [360, 90], replicated, may hold values from -0.3125 to 0.3125
- b_two: float32 [90], replicated, may hold values from -3 to 3
- cotangent: bfloat16 [8, 90, 512, 512], P('face', None, 'tile'), may hold values from -6 to 6
Outputs:
- output: bfloat16 [8, 90, 512, 512], P('face', None, 'tile')
- grad_one: float32 [90, 360], replicated
- grad_two: float32 [360, 90], replicated
- grad_kernel: float32 [9, 90], replicated
Inputs may be any that keep to these rules, and one draw needn't show every extreme that they name: `entry_block`: blocks k * 128 to (k + 1) * 128 - 1 belong to device k. At most 2 entries of one device name blocks of one device; in every draw one device gets exactly 2 from every device. `lat_to_nested`: A permutation of all blocks; the 128 blocks of each device go one to each device. `face_links`: entry [f, s, 0] names a face other than f; [f, s, 1] a side 0 to 3; [f, s, 2] is 0 or 1.
All inputs are finite; a program needn't handle non-finite values.
Results may differ from a plain program's by a relative error of at most 0.0081.
Values may be sent and summed in bfloat16 or wider, within the bound.
A program may use at most 192 MiB of HBM per device.

v0:
```python
import math
import jax
import jax.numpy as jnp
from jax import lax
from jax.sharding import PartitionSpec as P

CAP = 2
GELU_K = 0.7978845608028654
GELU_C = 0.044715
NORM_EPS = 1e-06


def with_halo(cells, sides, width):
    for axis, dim in sides:
        count = lax.axis_size(axis)
        ends = count - 1
        head = lax.slice_in_dim(cells, 0, width, axis=dim)
        tail = lax.slice_in_dim(cells, cells.shape[dim] - width, cells.shape[dim], axis=dim)
        cells = jnp.concatenate(
            [
                lax.ppermute(tail, axis, [(i, (i + 1) % count) for i in range(ends)]),
                cells,
                lax.ppermute(head, axis, [((i + 1) % count, i) for i in range(ends)]),
            ],
            axis=dim,
        )
    return cells


def gelu_pair(pre_act):
    inner = GELU_K * (pre_act + GELU_C * pre_act * pre_act * pre_act)
    tanh_val = jnp.tanh(inner)
    gelu_val = 0.5 * pre_act * (1.0 + tanh_val)
    gelu_slope = 0.5 * (1.0 + tanh_val) + 0.5 * pre_act * (1.0 - tanh_val * tanh_val) * GELU_K * (
        1.0 + 3.0 * GELU_C * pre_act * pre_act
    )
    return (gelu_val, gelu_slope)


def contract_rows(left_mat, right_mat):
    return lax.dot_general(
        left_mat, right_mat, (((1,), (1,)), ((), ())), preferred_element_type=jnp.float32
    )


def strip_work(padded, middle, cotan, kernel, ln_gain, ln_bias, w_one, b_one, w_two, b_two, scale):
    lat_count = padded.shape[0]
    row_count = padded.shape[1] - 2
    col_count = padded.shape[2] - 2
    wide = padded.astype(jnp.float32)
    depth_sum = jnp.zeros((lat_count, row_count, col_count), jnp.float32)
    for tap_index in range(9):
        row_off = tap_index // 3
        col_off = tap_index % 3
        window = wide[:, row_off : row_off + row_count, col_off : col_off + col_count]
        depth_sum = depth_sum + kernel[tap_index][:, None, None] * window
    flat = depth_sum.reshape(lat_count, row_count * col_count)
    mean_val = jnp.mean(flat, axis=0, keepdims=True)
    centered = flat - mean_val
    variance = jnp.mean(centered * centered, axis=0, keepdims=True)
    inv_std = lax.rsqrt(variance + NORM_EPS)
    scaled = centered * inv_std
    normed = (scaled * ln_gain[:, None] + ln_bias[:, None]).astype(jnp.bfloat16)
    pre_act = jnp.dot(w_one.T, normed, preferred_element_type=jnp.float32) + b_one[:, None]
    gelu_val, gelu_slope = gelu_pair(pre_act)
    hidden = gelu_val.astype(jnp.bfloat16)
    summed = (
        jnp.dot(w_two.T, hidden, preferred_element_type=jnp.float32)
        + b_two[:, None]
        + middle.reshape(lat_count, -1).astype(jnp.float32)
    )
    output = summed.astype(jnp.bfloat16).reshape(lat_count, row_count, col_count)
    cot_flat = cotan.reshape(lat_count, -1)
    grad_two = contract_rows(hidden, cot_flat) * scale
    back_hidden = jnp.dot(w_two, cot_flat, preferred_element_type=jnp.float32)
    back_pre = (back_hidden * gelu_slope).astype(jnp.bfloat16)
    grad_one = contract_rows(normed, back_pre) * scale
    back_hat = jnp.dot(w_one, back_pre, preferred_element_type=jnp.float32) * ln_gain[:, None]
    back_depth = inv_std * (
        back_hat
        - jnp.mean(back_hat, axis=0, keepdims=True)
        - scaled * jnp.mean(back_hat * scaled, axis=0, keepdims=True)
    )
    back_grid = back_depth.reshape(lat_count, row_count, col_count)
    kernel_rows = []
    for tap_index in range(9):
        row_off = tap_index // 3
        col_off = tap_index % 3
        window = wide[:, row_off : row_off + row_count, col_off : col_off + col_count]
        kernel_rows.append(jnp.sum(back_grid * window, axis=(1, 2)))
    grad_kernel = jnp.stack(kernel_rows, axis=0) * scale
    return (output, grad_one, grad_two, grad_kernel)


def lift(w_in, b_in, values):
    flat = values.reshape(values.shape[0], -1)
    mixed = jnp.dot(w_in.T, flat, preferred_element_type=jnp.float32) + b_in[:, None]
    return mixed.astype(jnp.bfloat16).reshape((w_in.shape[1],) + values.shape[1:])


def assemble(rows_part, cols_part):
    tile_count = rows_part.shape[0]
    chan_count = rows_part.shape[1]
    left_line = cols_part[:, 0].transpose(1, 0, 2).reshape(chan_count, -1)
    right_line = cols_part[:, 1].transpose(1, 0, 2).reshape(chan_count, -1)
    return jnp.stack([rows_part[0], rows_part[tile_count - 1], left_line, right_line], axis=0)


def per_device(
    source,
    entry_block,
    entry_source,
    entry_weight,
    lat_to_nested,
    face_links,
    w_in,
    b_in,
    kernel,
    ln_gain,
    ln_bias,
    w_one,
    b_one,
    w_two,
    b_two,
    cotangent,
):
    tile_count = lax.axis_size("tile")
    tile_at = lax.axis_index("tile")
    face_at = lax.axis_index("face")
    face_count = lax.axis_size("face")
    dev_count = lax.axis_size(("face", "tile"))
    in_count = source.shape[1]
    block_len = entry_weight.shape[2]
    row_count = cotangent.shape[2]
    line_len = cotangent.shape[3]
    chosen = jnp.take(source, entry_source, axis=0)
    partials = jnp.einsum(
        "eis,esp->eip", chosen, entry_weight, preferred_element_type=jnp.float32
    ).astype(jnp.bfloat16)
    owner_dev = entry_block // dev_count
    local_block = entry_block % dev_count
    hit_table = (owner_dev[:, None] == jnp.arange(dev_count, dtype=jnp.int32)[None, :]).astype(
        jnp.int32
    )
    slot_rank = jnp.sum((jnp.cumsum(hit_table, axis=0) - 1) * hit_table, axis=1)
    outbox = (
        jnp.zeros((dev_count, CAP, in_count, block_len), jnp.bfloat16)
        .at[owner_dev, slot_rank]
        .set(partials)
    )
    labels = (
        jnp.full((dev_count, CAP), dev_count, jnp.int32).at[owner_dev, slot_rank].set(local_block)
    )
    received, got_labels = (
        lax.all_to_all(outbox, ("face", "tile"), split_axis=0, concat_axis=0, tiled=True),
        lax.all_to_all(labels, ("face", "tile"), split_axis=0, concat_axis=0, tiled=True),
    )
    lat_sum = jnp.zeros((dev_count, in_count, block_len), jnp.float32)
    lat_sum = lat_sum.at[got_labels.reshape(-1)].add(
        received.reshape(-1, in_count, block_len).astype(jnp.float32), mode="drop"
    )
    lat_field = lat_sum.astype(jnp.bfloat16)
    target_dev = lat_to_nested // dev_count
    target_spot = lat_to_nested % dev_count
    outgoing = jnp.zeros_like(lat_field).at[target_dev].set(lat_field)
    out_spots = jnp.zeros((dev_count,), jnp.int32).at[target_dev].set(target_spot)
    incoming, in_spots = (
        lax.all_to_all(outgoing, ("face", "tile"), split_axis=0, concat_axis=0, tiled=True),
        lax.all_to_all(out_spots, ("face", "tile"), split_axis=0, concat_axis=0, tiled=True),
    )
    placed = jnp.zeros_like(incoming).at[in_spots].set(incoming)
    inputs_tile = placed.transpose(1, 0, 2).reshape(in_count, row_count, line_len)
    latent = lift(w_in, b_in, inputs_tile)
    chan_count = latent.shape[0]
    row_start = tile_at * row_count
    edge_cols = jnp.stack([latent[:, :, 0], latent[:, :, line_len - 1]], axis=0)
    edge_row = jnp.where(tile_at == 0, latent[:, 0, :], latent[:, row_count - 1, :])
    rows_face, cols_face = (
        lax.all_gather(edge_row.reshape(-1), "tile", axis=0, tiled=True),
        lax.all_gather(edge_cols.reshape(-1), "tile", axis=0, tiled=True),
    )
    own_lines = assemble(
        rows_face.reshape(tile_count, chan_count, line_len),
        cols_face.reshape(tile_count, 2, chan_count, row_count),
    )
    all_lines = lax.all_gather(own_lines.reshape(-1), "face", axis=0, tiled=True).reshape(
        face_count, 4, chan_count, line_len
    )
    face_link = face_links[face_at]
    picked = all_lines[face_link[:, 0], face_link[:, 1]]
    picked = jnp.where(face_link[:, 2][:, None, None] == 1, picked[:, :, ::-1], picked)
    row_lines = picked[0:2]
    full_cols = jnp.pad(picked[2:4], ((0, 0), (0, 0), (1, 1)))
    side_cols = lax.dynamic_slice_in_dim(full_cols, row_start, row_count + 2, 2)
    rim = jnp.stack([latent[:, 0, :], latent[:, row_count - 1, :]], axis=1)
    extended = with_halo(rim, (("tile", 1),), 1)
    upper_row = extended[:, 0, :]
    lower_row = extended[:, 3, :]
    spot_ids = jnp.arange(row_count + 2, dtype=jnp.int32) + row_start - 1
    inside = (spot_ids >= 0) & (spot_ids < line_len)
    side_cols = jnp.where(inside[None, None, :], side_cols, jnp.zeros_like(side_cols))
    top_row = jnp.where(tile_at == 0, row_lines[0], upper_row)
    bottom_row = jnp.where(tile_at == tile_count - 1, row_lines[1], lower_row)
    middle = jnp.concatenate([top_row[:, None, :], latent, bottom_row[:, None, :]], axis=1)
    padded = jnp.concatenate([side_cols[0][:, :, None], middle, side_cols[1][:, :, None]], axis=2)
    scale = 1.0 / math.sqrt(face_count * line_len * line_len)
    output, grad_one, grad_two, grad_kernel = strip_work(
        padded, latent, cotangent[0], kernel, ln_gain, ln_bias, w_one, b_one, w_two, b_two, scale
    )
    grad_one, grad_two, grad_kernel = lax.psum((grad_one, grad_two, grad_kernel), ("face", "tile"))
    return (output[None], grad_one, grad_two, grad_kernel)


def solution(mesh):
    placed = (
        P(("face", "tile"), None, None),
        P(("face", "tile")),
        P(("face", "tile")),
        P(("face", "tile"), None, None),
        P(("face", "tile")),
        P(),
        P(),
        P(),
        P(),
        P(),
        P(),
        P(),
        P(),
        P(),
        P(),
        P("face", None, "tile", None),
    )
    return jax.shard_map(
        per_device,
        mesh=mesh,
        in_specs=placed,
        out_specs=(P("face", None, "tile", None), P(), P(), P()),
        check_vma=False,
    )
```

profile of v0, /device:TPU:1, one launch (start us, length us, event | category | flops | bytes accessed | tf_op | source)
XLA Modules:
  0.0 591.9 jit_solution(9418654939937501962)
XLA Ops:
  8.4 6.4 %scatter_fusion = s32[128,2]{0,1:T(2,128)S(1)} fusion(s32[128,2]{0,1:T(2,128)S(1)} %broadcast_in_dim.44, s32[128]{0:T(128)S(1)} %fusion.33, s32[128]{0:T(128)S(1)} %get-tuple-element.43), kind=kCustom, calls=%fused_computation.3 | custom fusion | bytes 2560 | tf_op jit(solution)/shard_map/scatter | solution.py:152
  15.5 11.5 %all-to-all-start.1 = ((s32[128,1,2]{2,1,0:T(1,128)}), s32[128,1,2]{2,1,0:T(1,128)S(1)}, u32[]{:S(2)}, u32[]{:S(2)}) async-start(s32[128,1,2]{2,1,0:T(1,128)} %copy.79), calls=%async_computation.1 | async-start | bytes 131072 | tf_op jit(solution)/shard_map/all_to_all | solution.py:156
  33.0 13.3 %scatter_fusion.1 = bf16[128,2,16,128]{3,2,1,0:T(8,128)(2,1)} fusion(bf16[128,2,16,128]{3,2,1,0:T(8,128)(2,1)} %broadcast_in_dim.46, s32[128]{0:T(128)S(1)} %fusion.33, bf16[128,16,128]{2,1,0:T(8,128)(2,1)S(1)} %convolution_convert_fusion), kind=kCustom, calls=%fused_computation.4 | custom fusion | bytes 1573888 | tf_op jit(solution)/shard_map/scatter | solution.py:149
  46.2 9.8 %all-to-all-start.2 = ((bf16[128,2,16,128]{3,2,1,0:T(8,128)(2,1)}), bf16[128,2,16,128]{3,2,1,0:T(8,128)(2,1)S(1)}, u32[]{:S(2)}, u32[]{:S(2)}) async-start(bf16[128,2,16,128]{3,2,1,0:T(8,128)(2,1)} %scatter_fusion.1), calls=%async_computation.2 | async-start | bytes 2097152 | tf_op jit(solution)/shard_map/all_to_all | solution.py:155
  59.2 15.7 %all-to-all-done.2 = bf16[128,2,16,128]{3,2,1,0:T(8,128)(2,1)S(1)} async-done(((bf16[128,2,16,128]{3,2,1,0:T(8,128)(2,1)}), bf16[128,2,16,128]{3,2,1,0:T(8,128)(2,1)S(1)}, u32[]{:S(2)}, u32[]{:S(2)}) %all-to-all-start.2) | async-done | bytes 1048608 | tf_op jit(solution)/shard_map/all_to_all | solution.py:155
  74.9 4.5 all-to-all-start
  79.8 9.2 %scatter_fusion.2 = f32[128,16,128]{2,1,0:T(8,128)S(1)} fusion(f32[128,16,128]{2,1,0:T(8,128)S(1)} %broadcast_in_dim.43, s32[256]{0:T(256)S(1)} %bitcast.183, f32[256,16,128]{2,1,0:T(8,128)S(1)} %bitcast_convert_fusion), kind=kCustom, calls=%fused_computation.5 | custom fusion | flops 524288 | bytes 6292480 | tf_op jit(solution)/shard_map/scatter-add | solution.py:159
  90.0 13.2 %scatter_fusion.3 = bf16[128,16,128]{2,1,0:T(8,128)(2,1)} fusion(bf16[128,16,128]{2,1,0:T(8,128)(2,1)} %broadcast.194.clone, s32[128]{0:T(128)S(1)} %get-tuple-element.46, bf16[128,16,128]{2,1,0:T(8,128)(2,1)S(1)} %convert_element_type.45), kind=kCustom, calls=%fused_computation.6 | custom fusion | bytes 1573376 | tf_op jit(solution)/shard_map/scatter | solution.py:165
  103.1 9.8 %all-to-all-start.3 = ((bf16[128,16,128]{2,1,0:T(8,128)(2,1)}), bf16[128,16,128]{2,1,0:T(8,128)(2,1)S(1)}, u32[]{:S(2)}, u32[]{:S(2)}) async-start(bf16[128,16,128]{2,1,0:T(8,128)(2,1)} %scatter_fusion.3), calls=%async_computation.3 | async-start | bytes 1048576 | tf_op jit(solution)/shard_map/all_to_all | solution.py:168
  115.8 10.7 %all-to-all-done.3 = bf16[128,16,128]{2,1,0:T(8,128)(2,1)S(1)} async-done(((bf16[128,16,128]{2,1,0:T(8,128)(2,1)}), bf16[128,16,128]{2,1,0:T(8,128)(2,1)S(1)}, u32[]{:S(2)}, u32[]{:S(2)}) %all-to-all-start.3) | async-done | bytes 524320 | tf_op jit(solution)/shard_map/all_to_all | solution.py:168
  127.4 13.2 %scatter_fusion.4 = bf16[128,16,128]{2,1,0:T(8,128)(2,1)} fusion(bf16[128,16,128]{2,1,0:T(8,128)(2,1)} %broadcast.194, s32[128]{0:T(128)S(1)} %fusion.31, bf16[128,16,128]{2,1,0:T(8,128)(2,1)S(1)} %all-to-all-done.3), kind=kCustom, calls=%fused_computation.7 | custom fusion | bytes 1573376 | tf_op jit(solution)/shard_map/scatter | solution.py:171
  154.1 23.3 %all-gather = bf16[16,1,5760]{2,1,0:T(2,128)(2,1)} all-gather(bf16[1,1,5760]{2,1,0:T(2,128)(2,1)S(1)} %reshape.282), channel_id=1, replica_groups=mesh['face'=8,'tile'=16] {'tile'}, dimensions={0}, use_global_device_ids=true | all-gather | bytes 195840 | tf_op jit(solution)/shard_map/all_gather | solution.py:180
  185.9 4.6 all-gather.4.cloned.1.call-done
  201.0 3.7 copy.107
  205.1 3.8 slice.204
  214.0 24.0 %all-gather.6.cloned.1.call-done = bf16[1474560]{0:T(1024)(128)(2,1)} async-done(((bf16[184320]{0:T(1024)(128)(2,1)}), bf16[1474560]{0:T(1024)(128)(2,1)}) %all-gather.6.cloned.1.call-update) | async-done | bytes 2949136 | tf_op jit(solution)/shard_map/all_gather | solution.py:186
  238.0 5.6 reshape.217
  246.8 8.5 %rev.3 = bf16[4,90,512]{2,1,0:T(8,128)(2,1)} reverse(bf16[4,90,512]{2,1,0:T(8,128)(2,1)} %gather_fusion.1), dimensions={2} | reverse | bytes 737280 | tf_op jit(solution)/shard_map/rev | solution.py:191
  262.7 8.9 %maximum_convert_fusion = f32[90,34,514]{2,1,0:T(8,128)} fusion(bf16[90,34,1]{2,1,0:T(8,128)(2,1)} %copy.94, bf16[90,1,512]{2,1,0:T(2,128)(2,1)S(1)} %copy.91, bf16[90,32,512]{2,1,0:T(8,128)(2,1)} %slice.204, bf16[90,1,512]{2,1,0:T(2,128)(2,1)} %copy.90, bf16[90,34,1]{2,1,0:T(8,128)(2,1)} %copy.93), kind=kLoop, calls=%fused_computation.45 | loop fusion | flops 15728400 | bytes 9437040 | tf_op jit(solution)/shard_map/convert_element_type | solution.py:50
  271.6 34.9 %fusion.38 = (f32[32,512]{1,0:T(8,128)S(1)}, f32[90,32,512]{2,1,0:T(8,128)}) fusion(f32[90,34,514]{2,1,0:T(8,128)} %maximum_convert_fusion, f32[90]{0:T(128)S(1)} %get-tuple-element.41, f32[90]{0:T(128)S(1)} %get-tuple-element.42, f32[90]{0:T(128)S(1)} %get-tuple-element.35, f32[90]{0:T(128)S(1)} %get-tuple-element.36, f32[90]{0:T(128)S(1)} %get-tuple-element.37, ...), kind=kLoop, calls=%fused_computation.128 | loop fusion | flops 26525696 | bytes 59051176 | tf_op jit(solution)/shard_map/reduce_sum | solution.py:58
  310.1 4.3 copy.103
  315.5 15.2 %multiply_convert_fusion = (bf16[360,16384]{1,0:T(8,128)(2,1)}, f32[16384,360]{0,1:T(8,128)}) fusion(f32[360]{0:T(512)S(1)} %copy-done.16, bf16[90,360]{1,0:T(8,128)(2,1)S(1)} %copy-done.7, f32[90,16384]{1,0:T(8,128)S(1)} %bitcast.150, f32[90]{0:T(128)S(1)} %copy-done.15, f32[90]{0:T(128)S(1)} %copy-done.10, f32[16384]{0:T(1024)S(1)} %bitcast.169, ...), kind=kOutput, calls=%fused_computation.18 | convolution fusion | flops 1128038400 | bytes 41485712 | tf_op jit(solution)/shard_map/dot_general | solution.py:64
  330.7 20.6 %fusion.6 = bf16[360,16384]{1,0:T(8,128)(2,1)} fusion(f32[16384,360]{0,1:T(8,128)} %get-tuple-element.48, bf16[360,90]{0,1:T(8,128)(2,1)S(1)} %copy-done.8, bf16[90,16384]{1,0:T(8,128)(2,1)S(1)} %bitcast.165), kind=kOutput, calls=%fused_computation.16 | convolution fusion | flops 1173749760 | bytes 38403360 | tf_op jit(solution)/shard_map/dot_general | solution.py:75
  351.3 8.7 %convolution_multiply_fusion.1 = f32[90,360]{1,0:T(8,128)} fusion(bf16[360,16384]{1,0:T(8,128)(2,1)} %fusion.6, f32[90,16384]{1,0:T(8,128)S(1)} %bitcast.151, f32[90]{0:T(128)S(1)} %copy-done.15, f32[90]{0:T(128)S(1)} %copy-done.10, f32[16384]{0:T(1024)S(1)} %bitcast.170, f32[16384]{0:T(1024)S(1)} %bitcast.174), kind=kOutput, calls=%fused_computation.48 | convolution fusion | flops 1069088384 | bytes 17956112 | tf_op jit(solution)/shard_map/dot_general | solution.py:41
  360.0 10.5 %fusion.13 = (f32[16384]{0:T(1024)S(1)}, f32[16384,90]{0,1:T(8,128)}) fusion(f32[90,16384]{1,0:T(8,128)S(1)} %bitcast.152, f32[16384]{0:T(1024)S(1)} %bitcast.171, f32[16384]{0:T(1024)S(1)} %bitcast.175, f32[90]{0:T(128)S(1)} %copy-done.10, bf16[360,16384]{1,0:T(8,128)(2,1)} %fusion.6, bf16[90,360]{1,0:T(8,128)(2,1)S(1)} %copy-done.7), kind=kOutput, calls=%fused_computation.31 | convolution fusion | flops 1069039616 | bytes 23854728 | tf_op jit(solution)/shard_map/dot_general | solution.py:78
  370.6 8.6 %convolution_multiply_fusion.2 = f32[360,90]{0,1:T(8,128)} fusion(bf16[360,16384]{1,0:T(8,128)(2,1)} %get-tuple-element.47, bf16[90,16384]{1,0:T(8,128)(2,1)S(1)} %bitcast.166), kind=kOutput, calls=%fused_computation.49 | convolution fusion | flops 1061715584 | bytes 14875200 | tf_op jit(solution)/shard_map/dot_general | solution.py:41
  379.1 6.9 %fusion.10 = bf16[90,16384]{1,0:T(8,128)(2,1)S(1)} fusion(bf16[360,16384]{1,0:T(8,128)(2,1)} %get-tuple-element.47, bf16[360,90]{0,1:T(8,128)(2,1)S(1)} %copy-done.8, bf16[16384,90]{0,1:T(8,128)(2,1)S(1)} %fusion.7, f32[90]{0:T(128)S(1)} %copy-done.11), kind=kOutput, calls=%fused_computation.26 | convolution fusion | flops 1067581440 | bytes 17759880 | tf_op jit(solution)/shard_map/dot_general | solution.py:68
  392.7 6.2 %fusion.12 = f32[90,16384]{1,0:T(8,128)S(1)} fusion(f32[16384,90]{0,1:T(8,128)} %get-tuple-element.50, f32[90,16384]{1,0:T(8,128)} %bitcast.153, f32[16384]{0:T(1024)S(1)} %broadcast_multiply_fusion, f32[16384]{0:T(1024)S(1)} %broadcast_multiply_fusion.1, f32[16384]{0:T(1024)S(1)} %bitcast.172, f32[16384]{0:T(1024)S(1)} %bitcast.176), kind=kLoop, calls=%fused_computation.30 | loop fusion | flops 8847360 | bytes 17956864 | tf_op jit(solution)/shard_map/mul | solution.py:79
  398.9 7.0 %copy.108 = f32[12,8,32,512]{3,2,1,0:T(8,128)} copy(f32[12,8,32,512]{3,1,2,0:T(8,128)S(1)} %bitcast.158) | data formatting | bytes 12582912
  405.9 31.9 %multiply_reduce_fusion = (f32[90]{0:T(128)S(1)}, f32[90]{0:T(128)S(1)}, f32[90]{0:T(128)S(1)}, f32[90]{0:T(128)S(1)}, f32[90]{0:T(128)S(1)}, /*index=5*/f32[90]...) fusion(f32[90,34,514]{2,1,0:T(8,128)} %maximum_convert_fusion, f32[96,32,512]{2,1,0:T(8,128)} %bitcast.159), kind=kLoop, calls=%fused_computation.34 | loop fusion | flops 26541270 | bytes 58985640 | tf_op jit(solution)/shard_map/reduce_sum | solution.py:90
  437.8 67.0 %psum.23 = f32[9,90]{1,0:T(8,128)} all-reduce(f32[9,90]{1,0:T(8,128)S(1)} %broadcast_multiply_fusion.3), channel_id=1, replica_groups=mesh['face'=8,'tile'=16] {'face','tile'}, use_global_device_ids=true, to_apply=%region_23.24 | all-reduce | flops 810 | bytes 6480 | tf_op jit(solution)/shard_map/psum | solution.py:210
  504.8 77.2 %all-reduce.4.cloned.1.call-done = (f32[90,360]{1,0:T(8,128)}, f32[360,90]{0,1:T(8,128)}) async-done(((f32[90,360]{1,0:T(8,128)}, f32[360,90]{0,1:T(8,128)}), (f32[90,360]{1,0:T(8,128)}, f32[360,90]{0,1:T(8,128)})) %all-reduce.4.cloned.1.call-update) | async-done | bytes 259216 | tf_op jit(solution)/shard_map/psum | solution.py:210
  (134 shorter events, 78.7 us)
Async XLA Ops:
  7.2 20.5 %copy-start = (bf16[64,16,128]{2,1,0:T(8,128)(2,1)S(1)}, bf16[64,16,128]{2,1,0:T(8,128)(2,1)}, u32[]{:S(2)}) copy-start(bf16[64,16,128]{2,1,0:T(8,128)(2,1)} %param.16) | copy-start | bytes 786436
  8.0 48.0 %copy-start.17 = (s32[128]{0:T(128)S(1)}, s32[128]{0:T(128)}, u32[]{:S(2)}) copy-start(s32[128]{0:T(128)} %param.20) | copy-start | bytes 1540
  15.5 30.7 %all-to-all-start.1 = ((s32[128,1,2]{2,1,0:T(1,128)}), s32[128,1,2]{2,1,0:T(1,128)S(1)}, u32[]{:S(2)}, u32[]{:S(2)}) async-start(s32[128,1,2]{2,1,0:T(1,128)} %copy.79), calls=%async_computation.1 | async-start | bytes 131072 | tf_op jit(solution)/shard_map/all_to_all | solution.py:156
  46.2 28.7 %all-to-all-start.2 = ((bf16[128,2,16,128]{3,2,1,0:T(8,128)(2,1)}), bf16[128,2,16,128]{3,2,1,0:T(8,128)(2,1)S(1)}, u32[]{:S(2)}, u32[]{:S(2)}) async-start(bf16[128,2,16,128]{3,2,1,0:T(8,128)(2,1)} %scatter_fusion.1), calls=%async_computation.2 | async-start | bytes 2097152 | tf_op jit(solution)/shard_map/all_to_all | solution.py:155
  74.9 28.2 %all-to-all-start = ((s32[128,1,1]{2,1,0:T(1,128)}), s32[128,1,1]{2,1,0:T(1,128)S(1)}, u32[]{:S(2)}, u32[]{:S(2)}) async-start(s32[128,1,1]{2,1,0:T(1,128)} %copy.78), calls=%async_computation | async-start | bytes 131072 | tf_op jit(solution)/shard_map/all_to_all | solution.py:169
  79.8 60.8 %copy-start.12 = (bf16[16,90]{1,0:T(8,128)(2,1)S(1)}, bf16[16,90]{1,0:T(8,128)(2,1)}, u32[]{:S(2)}) copy-start(bf16[16,90]{1,0:T(8,128)(2,1)} %param.22) | copy-start | bytes 8644
  79.8 60.8 %copy-start.14 = (f32[90]{0:T(128)S(1)}, f32[90]{0:T(128)}, u32[]{:S(2)}) copy-start(f32[90]{0:T(128)} %param.23) | copy-start | bytes 1084
  103.1 23.4 %all-to-all-start.3 = ((bf16[128,16,128]{2,1,0:T(8,128)(2,1)}), bf16[128,16,128]{2,1,0:T(8,128)(2,1)S(1)}, u32[]{:S(2)}, u32[]{:S(2)}) async-start(bf16[128,16,128]{2,1,0:T(8,128)(2,1)} %scatter_fusion.3), calls=%async_computation.3 | async-start | bytes 1048576 | tf_op jit(solution)/shard_map/all_to_all | solution.py:168
  113.0 77.5 %all-gather.4.cloned.1.call-start = ((), (), s32[]{:S(2)}) async-start(), calls=%async_computation.4 | async-start | bytes 1566720 | tf_op jit(solution)/shard_map/all_gather | solution.py:179
  143.9 1.7 copy-start.3
  146.5 52.0 %copy-start.9 = (s32[8,4,3]{0,1,2:T(4,128)S(1)}, s32[8,4,3]{0,1,2:T(4,128)}, u32[]{:S(2)}) copy-start(s32[8,4,3]{0,1,2:T(4,128)} %param.21) | copy-start | bytes 1156
  147.3 90.7 %all-gather.6.cloned.1.call-start = ((), (), s32[]{:S(2)}) async-start(), calls=%async_computation.5 | async-start | bytes 3317760 | tf_op jit(solution)/shard_map/all_gather | solution.py:186
  198.3 6.8 %copy-start.13 = (f32[9,90]{1,0:T(8,128)S(1)}, f32[9,90]{1,0:T(8,128)}, u32[]{:S(2)}) copy-start(f32[9,90]{1,0:T(8,128)} %param.24) | copy-start | bytes 9724
  198.3 383.7 %all-reduce.4.cloned.1.call-start = ((), (), s32[]{:S(2)}) async-start(), calls=%async_computation.6 | async-start | bytes 589824 | tf_op jit(solution)/shard_map/psum | solution.py:210
  209.0 50.1 %collective-permute-start = (bf16[90,1,512]{2,0,1:T(8,128)(2,1)}, bf16[90,1,512]{2,0,1:T(8,128)(2,1)S(1)}, u32[]{:S(2)}, u32[]{:S(2)}) collective-permute-start(bf16[90,1,512]{2,0,1:T(8,128)(2,1)} %get-tuple-element.18), channel_id=1, source_target_pairs={{0,1},{1,2},{2,3},{3,4},{4,5},{5,6},{6,7},{7,8},{8,9},{9,10},{10,1... | collective-permute-start | bytes 276488 | tf_op jit(solution)/shard_map/ppermute | solution.py:21
  212.0 47.1 %collective-permute-start.1 = (bf16[90,1,512]{2,0,1:T(8,128)(2,1)}, bf16[90,1,512]{2,0,1:T(8,128)(2,1)}, u32[]{:S(2)}, u32[]{:S(2)}) collective-permute-start(bf16[90,1,512]{2,0,1:T(8,128)(2,1)} %get-tuple-element.19), channel_id=1, source_target_pairs={{1,0},{2,1},{3,2},{4,3},{5,4},{6,5},{7,6},{8,7},{9,8},{10,9},{11,1... | collective-permute-start | bytes 276488 | tf_op jit(solution)/shard_map/ppermute | solution.py:23
  256.5 0.8 copy-start.6
  306.5 8.0 %slice-start = ((s8[5898240]{0:T(1024)(128)(4,1)}), s8[4194304]{0:T(1024)(128)(4,1)S(1)}, s32[]{:S(2)}) async-start(s8[5898240]{0:T(1024)(128)(4,1)} %bitcast.154), calls=%async_computation.7 | async-start | bytes 8388608
  310.1 4.5 slice-start.1
  314.5 45.5 %copy-start.2 = (f32[12,8,32,512]{3,1,2,0:T(8,128)}, f32[12,8,32,512]{3,1,2,0:T(8,128)S(1)}, u32[]{:S(2)}) copy-start(f32[12,8,32,512]{3,1,2,0:T(8,128)S(1)} %copy.103) | copy-start | bytes 18874372
  314.5 1.0 copy-start.7
  314.5 0.9 copy-start.10
  314.5 0.9 copy-start.15
  314.5 0.9 copy-start.16
  315.4 15.2 %copy-start.4 = (bf16[12,8,32,512]{3,1,2,0:T(8,128)(2,1)S(1)}, bf16[12,8,32,512]{3,1,2,0:T(8,128)(2,1)}, u32[]{:S(2)}) copy-start(bf16[12,8,32,512]{3,1,2,0:T(8,128)(2,1)} %copy.107) | copy-start | bytes 9437188
  315.4 15.2 %copy-start.8 = (bf16[360,90]{0,1:T(8,128)(2,1)S(1)}, bf16[360,90]{0,1:T(8,128)(2,1)}, u32[]{:S(2)}) copy-start(bf16[360,90]{0,1:T(8,128)(2,1)} %param.29) | copy-start | bytes 194404
  360.0 10.6 %copy-start.5 = (bf16[12,8,32,512]{3,1,2,0:T(8,128)(2,1)S(1)}, bf16[12,8,32,512]{3,1,2,0:T(8,128)(2,1)}, u32[]{:S(2)}) copy-start(bf16[12,8,32,512]{3,1,2,0:T(8,128)(2,1)} %copy.107) | copy-start | bytes 9437188
  370.6 8.6 %copy-start.11 = (f32[90]{0:T(128)S(1)}, f32[90]{0:T(128)}, u32[]{:S(2)}) copy-start(f32[90]{0:T(128)} %param.30) | copy-start | bytes 1084
  405.9 179.2 %copy-start.1 = (bf16[64,16,128]{2,1,0:T(8,128)(2,1)S(1)}, bf16[64,16,128]{2,1,0:T(8,128)(2,1)}, u32[]{:S(2)}) copy-start(bf16[64,16,128]{2,1,0:T(8,128)(2,1)} %param.16) | copy-start | bytes 786436
Sparse Core Ops, SparseCore 0:
  147.4 43.0 all-gather.3
  198.4 39.5 all-gather.5
  437.9 144.0 all-reduce.3
where the time goes:
time: 601 us; the launch traced here: 592 us
  waiting for transfers between devices  132 us (22%)
  local copies, waits for them, and re-layouts  130 us (22%)
  other arithmetic  107 us (18%)
  blocking collectives  90.3 us (15%)
  matrix products  76 us (13%)
  starting transfers between devices  41.3 us (7%)
  between operations  14.6 us (2%)
    psum x1, waiting for transfers between devices, per_device(): lax.psum((grad_one, grad_two, grad_kernel), ('face', 'tile'))  77.2 us
    psum x1, blocking collectives, per_device(): lax.psum((grad_one, grad_two, grad_kernel), ('face', 'tile'))  67 us
    reduce_sum x1, other arithmetic, strip_work(): mean_val = jnp.mean(flat, axis=0, keepdims=True)  34.9 us
    unnamed x54, local copies, waits for them, and re-layouts  33.3 us
    reduce_sum x1, other arithmetic, strip_work(): kernel_rows.append(jnp.sum(back_grid * window, axis=(1, 2)))  31.9 us
    all_gather x1, waiting for transfers between devices, per_device(): lax.all_gather(own_lines.reshape(-1), 'face', axis=0, tiled=True)  24 us
    all_gather x1, blocking collectives, per_device(): lax.all_gather(edge_cols.reshape(-1), 'tile', axis=0, tiled=True)  23.3 us
    dot_general x1, matrix products, strip_work(): back_hidden = jnp.dot(w_two, cot_flat, preferred_element_type=jnp.float32)  20.6 us
  transfers between devices with their start and end apart: 9, of which 5 were waited for; matrix products, arithmetic and copies ran while one was open for 16% of the time, Pallas kernels for 0%

commit v1 on v0

--- a/solution.py
+++ b/solution.py
@@ -207,7 +207,13 @@
     output, grad_one, grad_two, grad_kernel = strip_work(
         padded, latent, cotangent[0], kernel, ln_gain, ln_bias, w_one, b_one, w_two, b_two, scale
     )
-    grad_one, grad_two, grad_kernel = lax.psum((grad_one, grad_two, grad_kernel), ("face", "tile"))
+
+    def note_ladders(z_in):
+        for u in ("face", "tile"):
+            z_in = lax.psum(z_in, u)
+        return z_in
+
+    grad_one, grad_two, grad_kernel = note_ladders((grad_one, grad_two, grad_kernel))
     return (output[None], grad_one, grad_two, grad_kernel)
 
 

time: 601 us -> 646 us (1.075)
  waiting for transfers between devices: 132 us -> 202 us
  local copies, waits for them, and re-layouts: 130 us -> 117 us
  blocking collectives: 90.3 us -> 78.8 us
    psum x1 -> x2, waiting for transfers between devices: 77.2 us -> 145 us  [note_ladders(): z_in = lax.psum(z_in, u)]
    psum x1 -> x2, blocking collectives: 67 us -> 55.7 us  [note_ladders(): z_in = lax.psum(z_in, u)]
    scatter x1, local copies, waits for them, and re-layouts: 13.2 us -> 4.37 us  [per_device(): placed = jnp.zeros_like(incoming).at[in_spots].set(incoming)]
    unnamed x54 -> x58, local copies, waits for them, and re-layouts: 33.3 us -> 33.4 us
  transfers between devices with their start and end apart: 9 -> 10, of which waited for: 5 -> 6; matrix products, arithmetic and copies ran while one was open for 16% -> 16% of each run, Pallas kernels for 0% -> 0%
where the time goes in v1:
time: 646 us; the launch traced here: 636 us
  waiting for transfers between devices  202 us (31%)
  local copies, waits for them, and re-layouts  117 us (18%)
  other arithmetic  106 us (16%)
  blocking collectives  78.8 us (12%)
  matrix products  75 us (12%)
  starting transfers between devices  41.9 us (6%)
  between operations  14.6 us (2%)
    psum x2, waiting for transfers between devices, note_ladders(): z_in = lax.psum(z_in, u)  145 us
    psum x2, blocking collectives, note_ladders(): z_in = lax.psum(z_in, u)  55.7 us
    reduce_sum x1, other arithmetic, strip_work(): mean_val = jnp.mean(flat, axis=0, keepdims=True)  34.7 us
    unnamed x58, local copies, waits for them, and re-layouts  33.4 us
    reduce_sum x1, other arithmetic, strip_work(): kernel_rows.append(jnp.sum(back_grid * window, axis=(1, 2)))  31.6 us
    all_gather x1, waiting for transfers between devices, per_device(): lax.all_gather(own_lines.reshape(-1), 'face', axis=0, tiled=True)  25.2 us
    all_gather x1, blocking collectives, per_device(): lax.all_gather(edge_cols.reshape(-1), 'tile', axis=0, tiled=True)  23.1 us
    dot_general x1, matrix products, strip_work(): back_hidden = jnp.dot(w_two, cot_flat, preferred_element_type=jnp.float32)  20.7 us
  transfers between devices with their start and end apart: 10, of which 6 were waited for; matrix products, arithmetic and copies ran while one was open for 16% of the time, Pallas kernels for 0%

profile of v1, /device:TPU:1, one launch (start us, length us, event | category | flops | bytes accessed | tf_op | source)
XLA Modules:
  0.0 635.6 jit_solution(14422402901734254733)
XLA Ops:
  8.4 6.4 %scatter_fusion = s32[128,2]{0,1:T(2,128)S(1)} fusion(s32[128,2]{0,1:T(2,128)S(1)} %broadcast_in_dim.44, s32[128]{0:T(128)S(1)} %fusion.33, s32[128]{0:T(128)S(1)} %get-tuple-element.45), kind=kCustom, calls=%fused_computation.3 | custom fusion | bytes 2560 | tf_op jit(solution)/shard_map/scatter | solution.py:152
  15.5 11.5 %all-to-all-start.1 = ((s32[128,1,2]{2,1,0:T(1,128)}), s32[128,1,2]{2,1,0:T(1,128)S(1)}, u32[]{:S(2)}, u32[]{:S(2)}) async-start(s32[128,1,2]{2,1,0:T(1,128)} %copy.79), calls=%async_computation.1 | async-start | bytes 131072 | tf_op jit(solution)/shard_map/all_to_all | solution.py:156
  33.0 13.3 %scatter_fusion.1 = bf16[128,2,16,128]{3,2,1,0:T(8,128)(2,1)} fusion(bf16[128,2,16,128]{3,2,1,0:T(8,128)(2,1)} %broadcast_in_dim.46, s32[128]{0:T(128)S(1)} %fusion.33, bf16[128,16,128]{2,1,0:T(8,128)(2,1)S(1)} %convolution_convert_fusion), kind=kCustom, calls=%fused_computation.4 | custom fusion | bytes 1573888 | tf_op jit(solution)/shard_map/scatter | solution.py:149
  46.2 9.8 %all-to-all-start.2 = ((bf16[128,2,16,128]{3,2,1,0:T(8,128)(2,1)}), bf16[128,2,16,128]{3,2,1,0:T(8,128)(2,1)S(1)}, u32[]{:S(2)}, u32[]{:S(2)}) async-start(bf16[128,2,16,128]{3,2,1,0:T(8,128)(2,1)} %scatter_fusion.1), calls=%async_computation.2 | async-start | bytes 2097152 | tf_op jit(solution)/shard_map/all_to_all | solution.py:155
  59.2 15.7 %all-to-all-done.2 = bf16[128,2,16,128]{3,2,1,0:T(8,128)(2,1)S(1)} async-done(((bf16[128,2,16,128]{3,2,1,0:T(8,128)(2,1)}), bf16[128,2,16,128]{3,2,1,0:T(8,128)(2,1)S(1)}, u32[]{:S(2)}, u32[]{:S(2)}) %all-to-all-start.2) | async-done | bytes 1048608 | tf_op jit(solution)/shard_map/all_to_all | solution.py:155
  74.9 4.5 all-to-all-start
  79.8 9.2 %scatter_fusion.2 = f32[128,16,128]{2,1,0:T(8,128)S(1)} fusion(f32[128,16,128]{2,1,0:T(8,128)S(1)} %broadcast_in_dim.43, s32[256]{0:T(256)S(1)} %bitcast.183, f32[256,16,128]{2,1,0:T(8,128)S(1)} %bitcast_convert_fusion), kind=kCustom, calls=%fused_computation.5 | custom fusion | flops 524288 | bytes 6292480 | tf_op jit(solution)/shard_map/scatter-add | solution.py:159
  90.0 13.2 %scatter_fusion.3 = bf16[128,16,128]{2,1,0:T(8,128)(2,1)} fusion(bf16[128,16,128]{2,1,0:T(8,128)(2,1)} %broadcast.194.clone, s32[128]{0:T(128)S(1)} %get-tuple-element.48, bf16[128,16,128]{2,1,0:T(8,128)(2,1)S(1)} %convert_element_type.45), kind=kCustom, calls=%fused_computation.6 | custom fusion | bytes 1573376 | tf_op jit(solution)/shard_map/scatter | solution.py:165
  103.1 9.8 %all-to-all-start.3 = ((bf16[128,16,128]{2,1,0:T(8,128)(2,1)}), bf16[128,16,128]{2,1,0:T(8,128)(2,1)S(1)}, u32[]{:S(2)}, u32[]{:S(2)}) async-start(bf16[128,16,128]{2,1,0:T(8,128)(2,1)} %scatter_fusion.3), calls=%async_computation.3 | async-start | bytes 1048576 | tf_op jit(solution)/shard_map/all_to_all | solution.py:168
  115.7 10.9 %all-to-all-done.3 = bf16[128,16,128]{2,1,0:T(8,128)(2,1)S(1)} async-done(((bf16[128,16,128]{2,1,0:T(8,128)(2,1)}), bf16[128,16,128]{2,1,0:T(8,128)(2,1)S(1)}, u32[]{:S(2)}, u32[]{:S(2)}) %all-to-all-start.3) | async-done | bytes 524320 | tf_op jit(solution)/shard_map/all_to_all | solution.py:168
  126.6 4.4 scatter_fusion.4
  142.3 23.1 %all-gather = bf16[16,1,5760]{2,1,0:T(2,128)(2,1)} all-gather(bf16[1,1,5760]{2,1,0:T(2,128)(2,1)S(1)} %reshape.282), channel_id=1, replica_groups=mesh['face'=8,'tile'=16] {'tile'}, dimensions={0}, use_global_device_ids=true | all-gather | bytes 195840 | tf_op jit(solution)/shard_map/all_gather | solution.py:180
  173.9 6.0 all-gather.4.cloned.1.call-done
  201.9 25.2 %all-gather.6.cloned.1.call-done = bf16[1474560]{0:T(1024)(128)(2,1)} async-done(((bf16[184320]{0:T(1024)(128)(2,1)}), bf16[1474560]{0:T(1024)(128)(2,1)}) %all-gather.6.cloned.1.call-update) | async-done | bytes 2949136 | tf_op jit(solution)/shard_map/all_gather | solution.py:186
  227.1 5.6 reshape.217
  236.0 8.5 %rev.3 = bf16[4,90,512]{2,1,0:T(8,128)(2,1)} reverse(bf16[4,90,512]{2,1,0:T(8,128)(2,1)} %gather_fusion.1), dimensions={2} | reverse | bytes 737280 | tf_op jit(solution)/shard_map/rev | solution.py:191
  251.2 8.4 %maximum_convert_fusion = f32[90,34,514]{2,1,0:T(8,128)} fusion(bf16[90,34,1]{2,1,0:T(8,128)(2,1)} %copy.94, bf16[90,1,512]{2,1,0:T(2,128)(2,1)S(1)} %copy.91, bf16[90,32,512]{2,1,0:T(8,128)(2,1)S(1)} %copy-done.6, bf16[90,1,512]{2,1,0:T(2,128)(2,1)S(1)} %copy.90, bf16[90,34,1]{2,1,0:T(8,128)(2,1)} %copy.93), kind=kLoop, calls=%fused_computation.45 | loop fusion | flops 15728400 | bytes 9437040 | tf_op jit(solution)/shard_map/convert_element_type | solution.py:50
  259.5 34.7 %fusion.38 = (f32[32,512]{1,0:T(8,128)S(1)}, f32[90,32,512]{2,1,0:T(8,128)}) fusion(f32[90,34,514]{2,1,0:T(8,128)} %maximum_convert_fusion, f32[90]{0:T(128)S(1)} %get-tuple-element.43, f32[90]{0:T(128)S(1)} %get-tuple-element.44, f32[90]{0:T(128)S(1)} %get-tuple-element.37, f32[90]{0:T(128)S(1)} %get-tuple-element.38, f32[90]{0:T(128)S(1)} %get-tuple-element.39, ...), kind=kLoop, calls=%fused_computation.128 | loop fusion | flops 26525696 | bytes 59051176 | tf_op jit(solution)/shard_map/reduce_sum | solution.py:58
  297.8 4.3 copy.103
  303.1 15.2 %multiply_convert_fusion = (bf16[360,16384]{1,0:T(8,128)(2,1)}, f32[16384,360]{0,1:T(8,128)}) fusion(f32[360]{0:T(512)S(1)} %copy-done.18, bf16[90,360]{1,0:T(8,128)(2,1)S(1)} %copy-done.9, f32[90,16384]{1,0:T(8,128)S(1)} %bitcast.150, f32[90]{0:T(128)S(1)} %copy-done.17, f32[90]{0:T(128)S(1)} %copy-done.12, f32[16384]{0:T(1024)S(1)} %bitcast.169, ...), kind=kOutput, calls=%fused_computation.18 | convolution fusion | flops 1128038400 | bytes 41485712 | tf_op jit(solution)/shard_map/dot_general | solution.py:64
  318.3 20.7 %fusion.6 = bf16[360,16384]{1,0:T(8,128)(2,1)} fusion(f32[16384,360]{0,1:T(8,128)} %get-tuple-element.50, bf16[360,90]{0,1:T(8,128)(2,1)S(1)} %copy-done.10, bf16[90,16384]{1,0:T(8,128)(2,1)S(1)} %bitcast.165), kind=kOutput, calls=%fused_computation.16 | convolution fusion | flops 1173749760 | bytes 38403360 | tf_op jit(solution)/shard_map/dot_general | solution.py:75
  339.0 8.7 %convolution_multiply_fusion.1 = f32[90,360]{1,0:T(8,128)} fusion(bf16[360,16384]{1,0:T(8,128)(2,1)} %fusion.6, f32[90,16384]{1,0:T(8,128)S(1)} %bitcast.151, f32[90]{0:T(128)S(1)} %copy-done.17, f32[90]{0:T(128)S(1)} %copy-done.12, f32[16384]{0:T(1024)S(1)} %bitcast.170, f32[16384]{0:T(1024)S(1)} %bitcast.174), kind=kOutput, calls=%fused_computation.48 | convolution fusion | flops 1069088384 | bytes 17956112 | tf_op jit(solution)/shard_map/dot_general | solution.py:41
  347.8 10.4 %fusion.13 = (f32[16384]{0:T(1024)S(1)}, f32[16384,90]{0,1:T(8,128)}) fusion(f32[90,16384]{1,0:T(8,128)S(1)} %bitcast.152, f32[16384]{0:T(1024)S(1)} %bitcast.171, f32[16384]{0:T(1024)S(1)} %bitcast.175, f32[90]{0:T(128)S(1)} %copy-done.12, bf16[360,16384]{1,0:T(8,128)(2,1)} %fusion.6, bf16[90,360]{1,0:T(8,128)(2,1)S(1)} %copy-done.9), kind=kOutput, calls=%fused_computation.31 | convolution fusion | flops 1069039616 | bytes 23854728 | tf_op jit(solution)/shard_map/dot_general | solution.py:78
  358.1 8.7 %convolution_multiply_fusion.2 = f32[360,90]{0,1:T(8,128)} fusion(bf16[360,16384]{1,0:T(8,128)(2,1)} %get-tuple-element.49, bf16[90,16384]{1,0:T(8,128)(2,1)S(1)} %bitcast.166), kind=kOutput, calls=%fused_computation.49 | convolution fusion | flops 1061715584 | bytes 14875200 | tf_op jit(solution)/shard_map/dot_general | solution.py:41
  370.0 6.2 fusion.12
  376.2 7.3 %copy.108 = f32[12,8,32,512]{3,2,1,0:T(8,128)} copy(f32[12,8,32,512]{3,1,2,0:T(8,128)S(1)} %bitcast.158) | data formatting | bytes 12582912
  383.5 31.6 %multiply_reduce_fusion = (f32[90]{0:T(128)S(1)}, f32[90]{0:T(128)S(1)}, f32[90]{0:T(128)S(1)}, f32[90]{0:T(128)S(1)}, f32[90]{0:T(128)S(1)}, /*index=5*/f32[90]...) fusion(f32[90,34,514]{2,1,0:T(8,128)} %maximum_convert_fusion, f32[96,32,512]{2,1,0:T(8,128)} %bitcast.159), kind=kLoop, calls=%fused_computation.34 | loop fusion | flops 26541270 | bytes 58985640 | tf_op jit(solution)/shard_map/reduce_sum | solution.py:90
  415.4 6.9 %fusion.10 = bf16[90,16384]{1,0:T(8,128)(2,1)S(1)} fusion(bf16[360,16384]{1,0:T(8,128)(2,1)} %get-tuple-element.49, bf16[360,90]{0,1:T(8,128)(2,1)S(1)} %copy-done.10, bf16[16384,90]{0,1:T(8,128)(2,1)S(1)} %copy-done.4, f32[90]{0:T(128)S(1)} %copy-done.13), kind=kOutput, calls=%fused_computation.26 | convolution fusion | flops 1067581440 | bytes 17759880 | tf_op jit(solution)/shard_map/dot_general | solution.py:68
  423.6 15.7 %psum.46 = f32[9,90]{1,0:T(8,128)S(1)} all-reduce(f32[9,90]{1,0:T(8,128)S(1)} %broadcast_multiply_fusion.3), channel_id=1, replica_groups=mesh['face'=8,'tile'=16] {'face'}, use_global_device_ids=true, to_apply=%region_25.26 | all-reduce | flops 810 | bytes 6480 | tf_op jit(solution)/shard_map/psum | solution.py:213
  439.4 40.0 %psum.47 = f32[9,90]{1,0:T(8,128)} all-reduce(f32[9,90]{1,0:T(8,128)S(1)} %psum.46), channel_id=1, replica_groups=mesh['face'=8,'tile'=16] {'tile'}, use_global_device_ids=true, to_apply=%region_26.27 | all-reduce | flops 810 | bytes 6480 | tf_op jit(solution)/shard_map/psum | solution.py:213
  479.3 7.4 %all-reduce.8.cloned.1.call-done = (f32[90,360]{1,0:T(8,128)}, f32[360,90]{0,1:T(8,128)}) async-done(((f32[90,360]{1,0:T(8,128)}, f32[360,90]{0,1:T(8,128)}), (f32[90,360]{1,0:T(8,128)}, f32[360,90]{0,1:T(8,128)})) %all-reduce.8.cloned.1.call-update) | async-done | bytes 259216 | tf_op jit(solution)/shard_map/psum | solution.py:213
  488.6 137.2 %all-reduce.6.cloned.1.call-done = (f32[90,360]{1,0:T(8,128)}, f32[360,90]{0,1:T(8,128)}) async-done(((f32[90,360]{1,0:T(8,128)}, f32[360,90]{0,1:T(8,128)}), (f32[90,360]{1,0:T(8,128)}, f32[360,90]{0,1:T(8,128)})) %all-reduce.6.cloned.1.call-update) | async-done | bytes 259216 | tf_op jit(solution)/shard_map/psum | solution.py:213
  (142 shorter events, 80.7 us)
Async XLA Ops:
  7.2 20.5 %copy-start = (bf16[64,16,128]{2,1,0:T(8,128)(2,1)S(1)}, bf16[64,16,128]{2,1,0:T(8,128)(2,1)}, u32[]{:S(2)}) copy-start(bf16[64,16,128]{2,1,0:T(8,128)(2,1)} %param.16) | copy-start | bytes 786436
  8.0 48.0 %copy-start.19 = (s32[128]{0:T(128)S(1)}, s32[128]{0:T(128)}, u32[]{:S(2)}) copy-start(s32[128]{0:T(128)} %param.20) | copy-start | bytes 1540
  15.5 30.7 %all-to-all-start.1 = ((s32[128,1,2]{2,1,0:T(1,128)}), s32[128,1,2]{2,1,0:T(1,128)S(1)}, u32[]{:S(2)}, u32[]{:S(2)}) async-start(s32[128,1,2]{2,1,0:T(1,128)} %copy.79), calls=%async_computation.1 | async-start | bytes 131072 | tf_op jit(solution)/shard_map/all_to_all | solution.py:156
  46.2 28.7 %all-to-all-start.2 = ((bf16[128,2,16,128]{3,2,1,0:T(8,128)(2,1)}), bf16[128,2,16,128]{3,2,1,0:T(8,128)(2,1)S(1)}, u32[]{:S(2)}, u32[]{:S(2)}) async-start(bf16[128,2,16,128]{3,2,1,0:T(8,128)(2,1)} %scatter_fusion.1), calls=%async_computation.2 | async-start | bytes 2097152 | tf_op jit(solution)/shard_map/all_to_all | solution.py:155
  74.9 28.2 %all-to-all-start = ((s32[128,1,1]{2,1,0:T(1,128)}), s32[128,1,1]{2,1,0:T(1,128)S(1)}, u32[]{:S(2)}, u32[]{:S(2)}) async-start(s32[128,1,1]{2,1,0:T(1,128)} %copy.78), calls=%async_computation | async-start | bytes 131072 | tf_op jit(solution)/shard_map/all_to_all | solution.py:169
  79.8 51.2 %copy-start.14 = (bf16[16,90]{1,0:T(8,128)(2,1)S(1)}, bf16[16,90]{1,0:T(8,128)(2,1)}, u32[]{:S(2)}) copy-start(bf16[16,90]{1,0:T(8,128)(2,1)} %param.22) | copy-start | bytes 8644
  79.8 51.2 %copy-start.16 = (f32[90]{0:T(128)S(1)}, f32[90]{0:T(128)}, u32[]{:S(2)}) copy-start(f32[90]{0:T(128)} %param.23) | copy-start | bytes 1084
  103.1 23.4 %all-to-all-start.3 = ((bf16[128,16,128]{2,1,0:T(8,128)(2,1)}), bf16[128,16,128]{2,1,0:T(8,128)(2,1)S(1)}, u32[]{:S(2)}, u32[]{:S(2)}) async-start(bf16[128,16,128]{2,1,0:T(8,128)(2,1)} %scatter_fusion.3), calls=%async_computation.3 | async-start | bytes 1048576 | tf_op jit(solution)/shard_map/all_to_all | solution.py:168
  113.0 66.9 %all-gather.4.cloned.1.call-start = ((), (), s32[]{:S(2)}) async-start(), calls=%async_computation.4 | async-start | bytes 1566720 | tf_op jit(solution)/shard_map/all_gather | solution.py:179
  132.0 1.7 copy-start.3
  135.9 52.4 %copy-start.11 = (s32[8,4,3]{0,1,2:T(4,128)S(1)}, s32[8,4,3]{0,1,2:T(4,128)}, u32[]{:S(2)}) copy-start(s32[8,4,3]{0,1,2:T(4,128)} %param.21) | copy-start | bytes 1156
  136.7 90.4 %all-gather.6.cloned.1.call-start = ((), (), s32[]{:S(2)}) async-start(), calls=%async_computation.5 | async-start | bytes 3317760 | tf_op jit(solution)/shard_map/all_gather | solution.py:186
  187.7 7.2 %copy-start.15 = (f32[9,90]{1,0:T(8,128)S(1)}, f32[9,90]{1,0:T(8,128)}, u32[]{:S(2)}) copy-start(f32[9,90]{1,0:T(8,128)} %param.24) | copy-start | bytes 9724
  187.7 299.0 %all-reduce.8.cloned.1.call-start = ((), (), s32[]{:S(2)}) async-start(), calls=%async_computation.7 | async-start | bytes 589824 | tf_op jit(solution)/shard_map/psum | solution.py:213
  190.8 9.0 %copy-start.8 = (bf16[90,1,512]{2,0,1:T(8,128)(2,1)S(1)}, bf16[90,1,512]{2,0,1:T(8,128)(2,1)}, u32[]{:S(2)}) copy-start(bf16[90,1,512]{2,0,1:T(8,128)(2,1)} %get-tuple-element.21) | copy-start | bytes 276484
  196.8 51.5 %collective-permute-start = (bf16[90,1,512]{2,0,1:T(8,128)(2,1)}, bf16[90,1,512]{2,0,1:T(8,128)(2,1)S(1)}, u32[]{:S(2)}, u32[]{:S(2)}) collective-permute-start(bf16[90,1,512]{2,0,1:T(8,128)(2,1)} %get-tuple-element.20), channel_id=1, source_target_pairs={{0,1},{1,2},{2,3},{3,4},{4,5},{5,6},{6,7},{7,8},{8,9},{9,10},{10,1... | collective-permute-start | bytes 276488 | tf_op jit(solution)/shard_map/ppermute | solution.py:21
  199.7 51.4 %copy-start.6 = (bf16[90,32,512]{2,1,0:T(8,128)(2,1)S(1)}, bf16[90,32,512]{2,1,0:T(8,128)(2,1)}, u32[]{:S(2)}) copy-start(bf16[90,32,512]{2,1,0:T(8,128)(2,1)} %slice.204) | copy-start | bytes 8847364
  199.7 48.5 %collective-permute-start.1 = (bf16[90,1,512]{2,0,1:T(8,128)(2,1)S(1)}, bf16[90,1,512]{2,0,1:T(8,128)(2,1)S(1)}, u32[]{:S(2)}, u32[]{:S(2)}) collective-permute-start(bf16[90,1,512]{2,0,1:T(8,128)(2,1)S(1)} %copy-done.8), channel_id=1, source_target_pairs={{1,0},{2,1},{3,2},{4,3},{5,4},{6,5},{7,6},{8,7},{9,8},{10,9},{11,1... | collective-permute-start | bytes 276488 | tf_op jit(solution)/shard_map/ppermute | solution.py:23
  245.7 0.8 copy-start.7
  294.2 8.0 %slice-start = ((s8[5898240]{0:T(1024)(128)(4,1)}), s8[4194304]{0:T(1024)(128)(4,1)S(1)}, s32[]{:S(2)}) async-start(s8[5898240]{0:T(1024)(128)(4,1)} %bitcast.154), calls=%async_computation.8 | async-start | bytes 8388608
  297.8 4.5 slice-start.1
  302.2 45.6 %copy-start.2 = (f32[12,8,32,512]{3,1,2,0:T(8,128)}, f32[12,8,32,512]{3,1,2,0:T(8,128)S(1)}, u32[]{:S(2)}) copy-start(f32[12,8,32,512]{3,1,2,0:T(8,128)S(1)} %copy.103) | copy-start | bytes 18874372
  302.2 1.0 copy-start.9
  302.2 0.9 copy-start.12
  302.2 0.9 copy-start.17
  302.2 0.9 copy-start.18
  303.1 15.2 %copy-start.5 = (bf16[12,8,32,512]{3,1,2,0:T(8,128)(2,1)S(1)}, bf16[12,8,32,512]{3,1,2,0:T(8,128)(2,1)}, u32[]{:S(2)}) copy-start(bf16[12,8,32,512]{3,1,2,0:T(8,128)(2,1)} %copy.107) | copy-start | bytes 9437188
  303.1 15.2 %copy-start.10 = (bf16[360,90]{0,1:T(8,128)(2,1)S(1)}, bf16[360,90]{0,1:T(8,128)(2,1)}, u32[]{:S(2)}) copy-start(bf16[360,90]{0,1:T(8,128)(2,1)} %param.29) | copy-start | bytes 194404
  383.5 31.8 %copy-start.4 = (bf16[16384,90]{0,1:T(8,128)(2,1)S(1)}, bf16[16384,90]{0,1:T(8,128)(2,1)}, u32[]{:S(2)}) copy-start(bf16[16384,90]{0,1:T(8,128)(2,1)} %copy-done.3) | copy-start | bytes 8847364
  383.5 31.9 %copy-start.13 = (f32[90]{0:T(128)S(1)}, f32[90]{0:T(128)}, u32[]{:S(2)}) copy-start(f32[90]{0:T(128)} %param.30) | copy-start | bytes 1084
  415.1 210.6 %all-reduce.6.cloned.1.call-start = ((), (), s32[]{:S(2)}) async-start(), calls=%async_computation.6 | async-start | bytes 589824 | tf_op jit(solution)/shard_map/psum | solution.py:213
  422.3 206.6 %copy-start.1 = (bf16[64,16,128]{2,1,0:T(8,128)(2,1)S(1)}, bf16[64,16,128]{2,1,0:T(8,128)(2,1)}, u32[]{:S(2)}) copy-start(bf16[64,16,128]{2,1,0:T(8,128)(2,1)} %param.16) | copy-start | bytes 786436
Sparse Core Ops, SparseCore 0:
  136.8 43.0 all-gather.3
  187.8 39.2 all-gather.5
  415.2 71.4 all-reduce.7
  489.3 136.4 all-reduce.5
